TPU v7x, 32 devices: a whole 2x2x4 slice. The times are simulated.
32 devices in a mesh: parts: 2 (over x), space: 16 (over z, y, core).
Axes of the slice: x: 2, y: 2, z: 4, core: 2. Of those that a mesh axis runs over, the one named last changes fastest.
Arguments:
- forward_field: float32 [2, 16, 128, 2048], P(None, 'parts', 'space'), parts along dimension 1, may hold values from -6 to 6
- adjoint_start: float32 [2, 16, 128, 2048], P(None, 'parts', 'space'), parts along dimension 1, may hold values from -45 to 45
- permittivity: float32 [256, 2048], P(('parts', 'space')), parts along dimension 0, may hold values from 1 to 6
- wavenumbers: float32 [16], P('parts'), parts along dimension 0, may hold values from 0.25 to 0.55
- monitor_cells: int32 [128], P('parts'), parts along dimension 0, may hold values from 0 to 262143
- pml_widths: int32 [8], P('parts'), parts along dimension 0, may hold values from 6 to 19
- owner_map: int32 [32, 16], P(('parts', 'space')), parts along dimension 0, may hold values from 0 to 15, each once within a row
Outputs:
- adjoint: float32 [2, 16, 128, 2048], P(None, 'parts', 'space'), parts along dimension 1
- design_grad: float32 [32, 16, 1024], P(('parts', 'space')), parts along dimension 0
There are 2 independent parts, one for each index of `parts`. A program takes and returns all parts, laid end to end along the dimension named above; each array names one. Nothing has to cross between parts.
Inputs may be any that keep to these rules, and one draw needn't show every extreme that they name: Each row of owner_map names every index 0 to 15 once.
All inputs are finite; a program needn't handle non-finite values.
Results may differ from a plain program's by a relative error of at most 0.00015.
Values sent between devices are 32-bit elements; how exact they have to be, the bound alone decides.
A program may use at most 64 MiB of HBM per device.

v0:
```python
import jax
import jax.numpy as jnp
from jax import lax
from jax.sharding import PartitionSpec as P

ITERS = 2


SIGMA_PEAK = 4.0
MONITOR_GAIN = 4.0


def with_halo(cells, sides, width):
    for axis, dim in sides:
        count = lax.axis_size(axis)
        ends = count - 1
        head = lax.slice_in_dim(cells, 0, width, axis=dim)
        tail = lax.slice_in_dim(cells, cells.shape[dim] - width, cells.shape[dim], axis=dim)
        cells = jnp.concatenate(
            [
                lax.ppermute(tail, axis, [(i, (i + 1) % count) for i in range(ends)]),
                cells,
                lax.ppermute(head, axis, [((i + 1) % count, i) for i in range(ends)]),
            ],
            axis=dim,
        )
    return cells


def stretch(coord, low_width, high_width, total):
    lower_part = jnp.maximum(low_width - coord, 0.0) / low_width
    upper_part = jnp.maximum(coord - (total - 1.0 - high_width), 0.0) / high_width
    damping = SIGMA_PEAK * (lower_part**3 + upper_part**3)
    denominator = 1.0 + damping * damping
    return (1.0 / denominator, -damping / denominator)


def operate(padded, eps_rows, wave_sq, first_row, total_rows, widths):
    row_count = padded.shape[2]
    col_count = padded.shape[3]
    row_ids = (first_row + jnp.arange(row_count)).astype(jnp.float32)
    cen_re, cen_im = stretch(row_ids, widths[0], widths[1], total_rows)
    face_re, face_im = stretch(row_ids[:-1] + 0.5, widths[0], widths[1], total_rows)
    q_re = cen_re[:, None] * padded[0] - cen_im[:, None] * padded[1]
    q_im = cen_re[:, None] * padded[1] + cen_im[:, None] * padded[0]
    d_re = q_re[:, 1:] - q_re[:, :-1]
    d_im = q_im[:, 1:] - q_im[:, :-1]
    f_re = face_re[:, None] * d_re - face_im[:, None] * d_im
    f_im = face_re[:, None] * d_im + face_im[:, None] * d_re
    along_re = f_re[:, 1:] - f_re[:, :-1]
    along_im = f_im[:, 1:] - f_im[:, :-1]
    middle = padded[:, :, 1:-1]
    col_ids = jnp.arange(col_count).astype(jnp.float32)
    cy_re, cy_im = stretch(col_ids, widths[2], widths[3], col_count)
    hy_re, hy_im = stretch(
        jnp.arange(col_count + 1).astype(jnp.float32) - 0.5, widths[2], widths[3], col_count
    )
    p_re = cy_re * middle[0] - cy_im * middle[1]
    p_im = cy_re * middle[1] + cy_im * middle[0]
    zero_col = jnp.zeros(p_re.shape[:-1] + (1,), jnp.float32)
    p_re = jnp.concatenate([zero_col, p_re, zero_col], axis=-1)
    p_im = jnp.concatenate([zero_col, p_im, zero_col], axis=-1)
    e_re = p_re[..., 1:] - p_re[..., :-1]
    e_im = p_im[..., 1:] - p_im[..., :-1]
    g_re = hy_re * e_re - hy_im * e_im
    g_im = hy_re * e_im + hy_im * e_re
    cross_re = g_re[..., 1:] - g_re[..., :-1]
    cross_im = g_im[..., 1:] - g_im[..., :-1]
    mass_term = wave_sq[:, None, None] * eps_rows[None]
    out_re = -(along_re + cross_re) - mass_term * middle[0]
    out_im = -(along_im + cross_im) - mass_term * middle[1]
    centre = row_ids[1:-1]
    inside = ((centre >= 0.0) & (centre <= total_rows - 1.0)).astype(jnp.float32)[:, None]
    return jnp.stack([out_re * inside, out_im * inside])


def monitor_counts(monitor_cells, first_row, row_count, col_count):
    cell_rows = monitor_cells // col_count
    cell_cols = monitor_cells % col_count
    rows_hot = (cell_rows[None, :] == (first_row + jnp.arange(row_count))[:, None]).astype(
        jnp.float32
    )
    cols_hot = (cell_cols[:, None] == jnp.arange(col_count)[None, :]).astype(jnp.float32)
    return jnp.dot(
        rows_hot, cols_hot, preferred_element_type=jnp.float32, precision=lax.Precision.HIGHEST
    )


def times_field(coef, field):
    c_re = coef[0][:, None, None]
    c_im = coef[1][:, None, None]
    return jnp.stack([c_re * field[0] - c_im * field[1], c_re * field[1] + c_im * field[0]])


def inner_product(left, right):
    return jnp.stack(
        [
            jnp.sum(left[0] * right[0] + left[1] * right[1], axis=(1, 2)),
            jnp.sum(left[0] * right[1] - left[1] * right[0], axis=(1, 2)),
        ]
    )


def energy(field):
    return jnp.sum(field[0] * field[0] + field[1] * field[1], axis=(1, 2))


def divide(top, bottom):
    denominator = bottom[0] * bottom[0] + bottom[1] * bottom[1]
    return jnp.stack(
        [
            (top[0] * bottom[0] + top[1] * bottom[1]) / denominator,
            (top[1] * bottom[0] - top[0] * bottom[1]) / denominator,
        ]
    )


def advance(norm_sq, tau_now, theta_now, eta_now, step_coef, direction, guide, solution):
    coef = theta_now * theta_now * divide(eta_now, step_coef)
    direction = guide + times_field(coef, direction)
    theta_new = jnp.sqrt(norm_sq) / tau_now
    shrink = 1.0 / (1.0 + theta_new * theta_new)
    tau_now = tau_now * theta_new * jnp.sqrt(shrink)
    eta_now = shrink * step_coef
    solution = solution + times_field(eta_now, direction)
    return (direction, tau_now, theta_new, eta_now, solution)


def local(
    forward_field, adjoint_start, permittivity, wavenumbers, monitor_cells, pml_widths, owner_map
):
    tile_count = lax.axis_size("space")
    rows_here = adjoint_start.shape[2]
    col_count = adjoint_start.shape[3]
    total_rows = rows_here * tile_count
    first = lax.axis_index("space") * rows_here
    widths = pml_widths.astype(jnp.float32)
    wave_sq = wavenumbers * wavenumbers
    counts = monitor_counts(monitor_cells, first, rows_here, col_count)
    source = MONITOR_GAIN * counts * jnp.stack([-forward_field[0], forward_field[1]])

    def apply_near(field):
        padded = with_halo(field, (("space", 2),), 1)
        return operate(padded, permittivity, wave_sq, first - 1, total_rows, widths)

    residual = source - apply_near(adjoint_start)
    image_now = apply_near(residual)
    solution = adjoint_start
    quasi = residual
    first_dir = residual
    search = image_now
    direction = jnp.zeros_like(residual)
    start_sq = lax.psum(energy(residual), "space")
    quasi_sq = start_sq
    tau_now = jnp.sqrt(start_sq)
    theta_now = jnp.zeros_like(start_sq)
    eta_now = jnp.zeros((2,) + start_sq.shape, jnp.float32)
    rho_now = jnp.stack([start_sq, jnp.zeros_like(start_sq)])
    for iteration in range(ITERS):
        step_coef = divide(rho_now, lax.psum(inner_product(residual, search), "space"))
        quasi = quasi - times_field(step_coef, image_now)
        first_sq = lax.psum(energy(quasi), "space")
        direction, tau_now, theta_now, eta_now, solution = advance(
            first_sq, tau_now, theta_now, eta_now, step_coef, direction, first_dir, solution
        )
        second_dir = first_dir - times_field(step_coef, search)
        second_image = apply_near(second_dir)
        quasi = quasi - times_field(step_coef, second_image)
        quasi_sq, rho_new = lax.psum((energy(quasi), inner_product(residual, quasi)), "space")
        direction, tau_now, theta_now, eta_now, solution = advance(
            quasi_sq, tau_now, theta_now, eta_now, step_coef, direction, second_dir, solution
        )
        if iteration + 1 < ITERS:
            ratio_coef = divide(rho_new, rho_now)
            rho_now = rho_new
            first_dir = quasi + times_field(ratio_coef, second_dir)
            image_now = apply_near(first_dir)
            search = image_now + times_field(
                ratio_coef, second_image + times_field(ratio_coef, search)
            )
    gradient = -2.0 * jnp.sum(
        wave_sq[:, None, None] * (solution[0] * forward_field[0] - solution[1] * forward_field[1]),
        axis=0,
    )
    blocks = (
        gradient.reshape(rows_here, tile_count, col_count // tile_count)
        .transpose(1, 0, 2)
        .reshape(tile_count, -1)
    )
    owners = owner_map[0]
    tile_ids = jnp.arange(tile_count)
    inverse = jnp.sum(
        (owners[None, :] == tile_ids[:, None]).astype(jnp.int32) * tile_ids[None, :], axis=1
    )
    ordered = jnp.take(blocks, inverse, axis=0)
    received = lax.all_to_all(ordered, "space", split_axis=0, concat_axis=0, tiled=True)
    return (solution, received[None])


def solution(mesh):
    placed = (
        P(None, "parts", "space", None),
        P(None, "parts", "space", None),
        P(("parts", "space"), None),
        P("parts"),
        P("parts"),
        P("parts"),
        P(("parts", "space"), None),
    )
    return jax.shard_map(
        local,
        mesh=mesh,
        in_specs=placed,
        out_specs=(P(None, "parts", "space", None), P(("parts", "space"), None, None)),
        check_vma=False,
    )
```

profile of v0, /device:TPU:0, one launch (start us, length us, event | category | flops | bytes accessed | tf_op | source)
XLA Modules:
  0.0 207.9 jit_solution(9488998989571998975)
XLA Ops:
  0.7 1.8 fusion.113
  2.5 1.3 collective-permute-start.1
  3.8 3.0 %collective-permute-start = (f32[2,8,1,2048]{3,2,1,0:T(1,128)S(1)}, f32[2,8,1,2048]{3,2,1,0:T(1,128)S(1)}, u32[]{:S(2)}, u32[]{:S(2)}) collective-permute-start(f32[2,8,1,2048]{3,2,1,0:T(1,128)S(1)} %get-tuple-element.135), channel_id=1, source_target_pairs={{0,1},{1,2},{2,3},{3,4},{4,5},{5,6},{6,7},{7,8},{8,9},{9,10},{10,1... | collective-permute-start | bytes 393224 | tf_op jit(solution)/shard_map/ppermute | solution.py:21
  6.8 0.7 convert_element_type.59
  7.5 0.7 fusion.114
  8.8 1.3 negate_divide_fusion.1
  10.1 1.3 negate_divide_fusion
  12.0 1.3 fusion.98
  13.3 1.3 fusion.97
  14.7 1.3 slice_negate_fusion
  17.7 0.5 multiply_subtract_fusion.8
  18.6 0.5 fusion.6
  20.2 1.3 collective-permute-start.3
  21.5 5.1 %collective-permute-start.2 = (f32[2,8,1,2048]{3,2,1,0:T(1,128)S(1)}, f32[2,8,1,2048]{3,2,1,0:T(1,128)S(1)}, u32[]{:S(2)}, u32[]{:S(2)}) collective-permute-start(f32[2,8,1,2048]{3,2,1,0:T(1,128)S(1)} %get-tuple-element.133), channel_id=1, source_target_pairs={{0,1},{1,2},{2,3},{3,4},{4,5},{5,6},{6,7},{7,8},{8,9},{9,10},{10,1... | collective-permute-start | bytes 393224 | tf_op jit(solution)/shard_map/ppermute | solution.py:21
  27.0 0.6 collective-permute-done.2
  28.3 0.5 multiply_add_fusion.6
  28.8 0.8 add_reduce_fusion.2
  29.6 34.1 %all-reduce.21 = (f32[8]{0:T(128)S(1)}, f32[2,8]{1,0:T(2,128)S(1)}) all-reduce(f32[8]{0:T(128)S(1)} %get-tuple-element.13, f32[2,8]{1,0:T(2,128)S(1)} %pad_maximum_fusion.5), channel_id=1, replica_groups=mesh['parts'=2,'space'=16] {'space'}, use_global_device_ids=true, to_apply=%region_1.2 | all-reduce | flops 24 | bytes 192 | tf_op jit(solution)/shard_map/psum | solution.py:153
  64.3 0.5 copy-done.14
  65.0 1.3 maximum_subtract_fusion
  66.6 1.3 collective-permute-start.5
  67.9 3.0 %collective-permute-start.4 = (f32[2,8,1,2048]{3,2,1,0:T(1,128)S(1)}, f32[2,8,1,2048]{3,2,1,0:T(1,128)S(1)}, u32[]{:S(2)}, u32[]{:S(2)}) collective-permute-start(f32[2,8,1,2048]{3,2,1,0:T(1,128)S(1)} %get-tuple-element.129), channel_id=1, source_target_pairs={{0,1},{1,2},{2,3},{3,4},{4,5},{5,6},{6,7},{7,8},{8,9},{9,10},{10,1... | collective-permute-start | bytes 393224 | tf_op jit(solution)/shard_map/ppermute | solution.py:21
  71.3 0.6 collective-permute-done.4
  73.1 0.6 subtract_bitcast_fusion.3
  74.0 0.5 copy-done.17
  75.1 30.7 %psum.60 = f32[2,8]{1,0:T(2,128)S(1)} all-reduce(f32[2,8]{1,0:T(2,128)S(1)} %pad_maximum_fusion.7), channel_id=1, replica_groups=mesh['parts'=2,'space'=16] {'space'}, use_global_device_ids=true, to_apply=%region_11.12 | all-reduce | flops 16 | bytes 128 | tf_op jit(solution)/shard_map/psum | solution.py:169
  105.8 1.5 subtract_bitcast_fusion.2
  108.0 0.6 copy-done.2
  109.0 1.3 collective-permute-start.7
  110.3 3.2 %collective-permute-start.6 = (f32[2,8,1,2048]{3,2,1,0:T(1,128)S(1)}, f32[2,8,1,2048]{3,2,1,0:T(1,128)S(1)}, u32[]{:S(2)}, u32[]{:S(2)}) collective-permute-start(f32[2,8,1,2048]{3,2,1,0:T(1,128)S(1)} %get-tuple-element.126), channel_id=1, source_target_pairs={{0,1},{1,2},{2,3},{3,4},{4,5},{5,6},{6,7},{7,8},{8,9},{9,10},{10,1... | collective-permute-start | bytes 393224 | tf_op jit(solution)/shard_map/ppermute | solution.py:21
  115.5 0.5 fusion.19
  117.4 30.6 %psum.61 = f32[2,8]{1,0:T(2,128)S(1)} all-reduce(f32[2,8]{1,0:T(2,128)S(1)} %pad_maximum_fusion.8), channel_id=1, replica_groups=mesh['parts'=2,'space'=16] {'space'}, use_global_device_ids=true, to_apply=%region_14.15 | all-reduce | flops 16 | bytes 128 | tf_op jit(solution)/shard_map/psum | solution.py:160
  148.0 1.4 multiply_subtract_fusion.18
  149.8 0.5 copy-done.7
  150.7 1.3 collective-permute-start.9
  152.0 3.0 %collective-permute-start.8 = (f32[2,8,1,2048]{3,2,1,0:T(1,128)S(1)}, f32[2,8,1,2048]{3,2,1,0:T(1,128)S(1)}, u32[]{:S(2)}, u32[]{:S(2)}) collective-permute-start(f32[2,8,1,2048]{3,2,1,0:T(1,128)S(1)} %get-tuple-element.124), channel_id=1, source_target_pairs={{0,1},{1,2},{2,3},{3,4},{4,5},{5,6},{6,7},{7,8},{8,9},{9,10},{10,1... | collective-permute-start | bytes 393224 | tf_op jit(solution)/shard_map/ppermute | solution.py:21
  155.4 0.6 collective-permute-done.8
  156.8 0.5 multiply_subtract_fusion
  157.3 0.5 copy-done.22
  157.9 0.7 subtract_bitcast_fusion.1
  159.5 30.6 %all-reduce.20 = (f32[8]{0:T(128)S(1)}, f32[8]{0:T(128)S(1)}, f32[8]{0:T(128)S(1)}, f32[8]{0:T(128)S(1)}) all-reduce(f32[8]{0:T(128)S(1)} %get-tuple-element.128, f32[8]{0:T(128)S(1)} %get-tuple-element.12, f32[8]{0:T(128)S(1)} %fusion.37, f32[8]{0:T(128)S(1)} %fusion.31), channel_id=1, replica_groups=mesh['parts'=2,'space'=16] {'space'}, use_global_device_ids=true, to_apply=%region_6.7 | all-reduce | flops 32 | bytes 256 | tf_op jit(solution)/shard_map/psum | solution.py:162
  190.4 1.5 multiply_subtract_fusion.25
  193.1 0.7 copy-done.8
  194.5 1.0 copy-done.1
  195.9 0.8 copy-done.25
  197.0 0.6 gather_fusion
  197.7 9.5 %all_to_all.6 = f32[16,1,1024]{2,1,0:T(1,128)S(1)} all-to-all(f32[16,1,1024]{2,1,0:T(1,128)S(1)} %copy.11), channel_id=1, replica_groups=mesh['parts'=2,'space'=16] {'space'}, dimensions={0} | all-to-all | bytes 131072 | tf_op jit(solution)/shard_map/all_to_all | solution.py:196
  207.2 0.6 copy.12
  (155 shorter events, 17.7 us)
Async XLA Ops:
  0.6 15.6 %copy-start = (f32[2,8,8,2048]{3,2,1,0:T(8,128)S(1)}, f32[2,8,8,2048]{3,2,1,0:T(8,128)}, u32[]{:S(2)}) copy-start(f32[2,8,8,2048]{3,2,1,0:T(8,128)} %param.8) | copy-start | bytes 3145732
  0.6 15.4 %copy-start.28 = (f32[8]{0:T(128)S(1)}, f32[8]{0:T(128)}, u32[]{:S(2)}) copy-start(f32[8]{0:T(128)} %param.10) | copy-start | bytes 100
  0.7 15.4 %copy-start.29 = (s32[64]{0:T(128)S(1)}, s32[64]{0:T(128)}, u32[]{:S(2)}) copy-start(s32[64]{0:T(128)} %param.11) | copy-start | bytes 772
  0.7 15.4 %copy-start.30 = (s32[1,16]{1,0:T(1,128)S(1)}, s32[1,16]{1,0:T(1,128)}, u32[]{:S(2)}) copy-start(s32[1,16]{1,0:T(1,128)} %param.13) | copy-start | bytes 196
  2.5 14.5 %collective-permute-start.1 = (f32[2,8,1,2048]{3,2,1,0:T(1,128)S(1)}, f32[2,8,1,2048]{3,2,1,0:T(1,128)S(1)}, u32[]{:S(2)}, u32[]{:S(2)}) collective-permute-start(f32[2,8,1,2048]{3,2,1,0:T(1,128)S(1)} %get-tuple-element.136), channel_id=1, source_target_pairs={{1,0},{2,1},{3,2},{4,3},{5,4},{6,5},{7,6},{8,7},{9,8},{10,9},{11,1... | collective-permute-start | bytes 393224 | tf_op jit(solution)/shard_map/ppermute | solution.py:23
  3.8 13.2 %collective-permute-start = (f32[2,8,1,2048]{3,2,1,0:T(1,128)S(1)}, f32[2,8,1,2048]{3,2,1,0:T(1,128)S(1)}, u32[]{:S(2)}, u32[]{:S(2)}) collective-permute-start(f32[2,8,1,2048]{3,2,1,0:T(1,128)S(1)} %get-tuple-element.135), channel_id=1, source_target_pairs={{0,1},{1,2},{2,3},{3,4},{4,5},{5,6},{6,7},{7,8},{8,9},{9,10},{10,1... | collective-permute-start | bytes 393224 | tf_op jit(solution)/shard_map/ppermute | solution.py:21
  17.7 0.8 copy-start.27
  19.1 0.8 copy-start.13
  19.1 1.0 copy-start.15
  20.2 6.8 %collective-permute-start.3 = (f32[2,8,1,2048]{3,2,1,0:T(1,128)S(1)}, f32[2,8,1,2048]{3,2,1,0:T(1,128)S(1)}, u32[]{:S(2)}, u32[]{:S(2)}) collective-permute-start(f32[2,8,1,2048]{3,2,1,0:T(1,128)S(1)} %get-tuple-element.134), channel_id=1, source_target_pairs={{1,0},{2,1},{3,2},{4,3},{5,4},{6,5},{7,6},{8,7},{9,8},{10,9},{11,1... | collective-permute-start | bytes 393224 | tf_op jit(solution)/shard_map/ppermute | solution.py:23
  21.5 6.1 %collective-permute-start.2 = (f32[2,8,1,2048]{3,2,1,0:T(1,128)S(1)}, f32[2,8,1,2048]{3,2,1,0:T(1,128)S(1)}, u32[]{:S(2)}, u32[]{:S(2)}) collective-permute-start(f32[2,8,1,2048]{3,2,1,0:T(1,128)S(1)} %get-tuple-element.133), channel_id=1, source_target_pairs={{0,1},{1,2},{2,3},{3,4},{4,5},{5,6},{6,7},{7,8},{8,9},{9,10},{10,1... | collective-permute-start | bytes 393224 | tf_op jit(solution)/shard_map/ppermute | solution.py:21
  29.6 34.6 %copy-start.11 = (f32[8,8,2048]{2,1,0:T(8,128)}, f32[8,8,2048]{2,1,0:T(8,128)S(1)}, u32[]{:S(2)}) copy-start(f32[8,8,2048]{2,1,0:T(8,128)S(1)} %get-tuple-element.42) | copy-start | bytes 1572868
  29.6 34.6 %copy-start.12 = (f32[8,8,2048]{2,1,0:T(8,128)}, f32[8,8,2048]{2,1,0:T(8,128)S(1)}, u32[]{:S(2)}) copy-start(f32[8,8,2048]{2,1,0:T(8,128)S(1)} %get-tuple-element.43) | copy-start | bytes 1572868
  63.8 1.0 copy-start.14
  63.8 1.2 copy-start.16
  66.6 4.7 %collective-permute-start.5 = (f32[2,8,1,2048]{3,2,1,0:T(1,128)S(1)}, f32[2,8,1,2048]{3,2,1,0:T(1,128)S(1)}, u32[]{:S(2)}, u32[]{:S(2)}) collective-permute-start(f32[2,8,1,2048]{3,2,1,0:T(1,128)S(1)} %get-tuple-element.130), channel_id=1, source_target_pairs={{1,0},{2,1},{3,2},{4,3},{5,4},{6,5},{7,6},{8,7},{9,8},{10,9},{11,1... | collective-permute-start | bytes 393224 | tf_op jit(solution)/shard_map/ppermute | solution.py:23
  67.9 4.0 %collective-permute-start.4 = (f32[2,8,1,2048]{3,2,1,0:T(1,128)S(1)}, f32[2,8,1,2048]{3,2,1,0:T(1,128)S(1)}, u32[]{:S(2)}, u32[]{:S(2)}) collective-permute-start(f32[2,8,1,2048]{3,2,1,0:T(1,128)S(1)} %get-tuple-element.129), channel_id=1, source_target_pairs={{0,1},{1,2},{2,3},{3,4},{4,5},{5,6},{6,7},{7,8},{8,9},{9,10},{10,1... | collective-permute-start | bytes 393224 | tf_op jit(solution)/shard_map/ppermute | solution.py:21
  73.8 0.8 copy-start.17
  73.8 1.0 copy-start.19
  105.7 1.5 copy-start.18
  105.7 1.5 copy-start.20
  107.7 0.8 copy-start.2
  107.7 1.0 copy-start.4
  109.0 4.9 %collective-permute-start.7 = (f32[2,8,1,2048]{3,2,1,0:T(1,128)S(1)}, f32[2,8,1,2048]{3,2,1,0:T(1,128)S(1)}, u32[]{:S(2)}, u32[]{:S(2)}) collective-permute-start(f32[2,8,1,2048]{3,2,1,0:T(1,128)S(1)} %get-tuple-element.127), channel_id=1, source_target_pairs={{1,0},{2,1},{3,2},{4,3},{5,4},{6,5},{7,6},{8,7},{9,8},{10,9},{11,1... | collective-permute-start | bytes 393224 | tf_op jit(solution)/shard_map/ppermute | solution.py:23
  110.3 4.0 %collective-permute-start.6 = (f32[2,8,1,2048]{3,2,1,0:T(1,128)S(1)}, f32[2,8,1,2048]{3,2,1,0:T(1,128)S(1)}, u32[]{:S(2)}, u32[]{:S(2)}) collective-permute-start(f32[2,8,1,2048]{3,2,1,0:T(1,128)S(1)} %get-tuple-element.126), channel_id=1, source_target_pairs={{0,1},{1,2},{2,3},{3,4},{4,5},{5,6},{6,7},{7,8},{8,9},{9,10},{10,1... | collective-permute-start | bytes 393224 | tf_op jit(solution)/shard_map/ppermute | solution.py:21
  116.0 0.8 copy-start.21
  116.0 1.0 copy-start.23
  116.2 1.2 copy-start.6
  117.4 32.1 %copy-start.3 = (f32[1,8,8,2048]{3,2,1,0:T(8,128)S(1)}, f32[1,8,8,2048]{3,2,1,0:T(8,128)}, u32[]{:S(2)}) copy-start(f32[1,8,8,2048]{3,2,1,0:T(8,128)} %copy-done.2) | copy-start | bytes 1572868
  117.4 32.1 %copy-start.5 = (f32[1,8,8,2048]{3,2,1,0:T(8,128)S(1)}, f32[1,8,8,2048]{3,2,1,0:T(8,128)}, u32[]{:S(2)}) copy-start(f32[1,8,8,2048]{3,2,1,0:T(8,128)} %copy-done.4) | copy-start | bytes 1572868
  149.4 0.8 copy-start.7
  149.4 1.0 copy-start.9
  150.7 4.7 %collective-permute-start.9 = (f32[2,8,1,2048]{3,2,1,0:T(1,128)S(1)}, f32[2,8,1,2048]{3,2,1,0:T(1,128)S(1)}, u32[]{:S(2)}, u32[]{:S(2)}) collective-permute-start(f32[2,8,1,2048]{3,2,1,0:T(1,128)S(1)} %get-tuple-element.125), channel_id=1, source_target_pairs={{1,0},{2,1},{3,2},{4,3},{5,4},{6,5},{7,6},{8,7},{9,8},{10,9},{11,1... | collective-permute-start | bytes 393224 | tf_op jit(solution)/shard_map/ppermute | solution.py:23
  152.0 4.0 %collective-permute-start.8 = (f32[2,8,1,2048]{3,2,1,0:T(1,128)S(1)}, f32[2,8,1,2048]{3,2,1,0:T(1,128)S(1)}, u32[]{:S(2)}, u32[]{:S(2)}) collective-permute-start(f32[2,8,1,2048]{3,2,1,0:T(1,128)S(1)} %get-tuple-element.124), channel_id=1, source_target_pairs={{0,1},{1,2},{2,3},{3,4},{4,5},{5,6},{6,7},{7,8},{8,9},{9,10},{10,1... | collective-permute-start | bytes 393224 | tf_op jit(solution)/shard_map/ppermute | solution.py:21
  156.7 1.0 copy-start.22
  156.8 1.2 copy-start.24
  192.7 1.0 copy-start.8
  192.7 1.2 copy-start.10
  194.3 1.2 copy-start.1
  195.5 1.2 copy-start.25
  196.7 11.1 %copy-start.26 = (f32[2,8,8,2048]{3,2,1,0:T(8,128)}, f32[2,8,8,2048]{3,2,1,0:T(8,128)S(1)}, u32[]{:S(2)}) copy-start(f32[2,8,8,2048]{3,2,1,0:T(8,128)S(1)} %fusion.3) | copy-start | bytes 3145732
where the time goes:
time: 209 us; the launch traced here: 208 us
  blocking collectives  135 us (65%)
  other arithmetic  30.4 us (15%)
  starting transfers between devices  23.9 us (11%)
  local copies, waits for them, and re-layouts  12.7 us (6%)
  between operations  2.97 us (1%)
  waiting for transfers between devices  2.17 us (1%)
    psum x1, blocking collectives, local(): start_sq = lax.psum(energy(residual), 'space')  34.1 us
    psum x1, blocking collectives, local(): lax.psum((energy(quasi), inner_product(residual, quasi)), 'space')  30.7 us
    psum x1, blocking collectives, local(): lax.psum(inner_product(residual, search), 'space')  30.6 us
    psum x1, blocking collectives, local(): first_sq = lax.psum(energy(quasi), 'space')  30.6 us
    ppermute x5, starting transfers between devices, with_halo(): lax.ppermute(tail, axis, [(i, (i + 1) % count) for i in range(ends)])  17.5 us
    all_to_all x1, blocking collectives, local(): lax.all_to_all(ordered, 'space', split_axis=0, concat_axis=0, tiled=True)  9.48 us
    unnamed x64, local copies, waits for them, and re-layouts  8.72 us
    ppermute x5, starting transfers between devices, with_halo(): lax.ppermute(head, axis, [((i + 1) % count, i) for i in range(ends)])  6.46 us
  transfers between devices with their start and end apart: 10, of which 4 were waited for; matrix products, arithmetic and copies ran while one was open for 5% of the time, Pallas kernels for 0%

commit v1 on v0

v1 whole, which is shorter than its diff:
```python
import functools

import jax
import jax.numpy as jnp
from jax import lax
from jax.experimental import pallas as pl
from jax.experimental.pallas import tpu as pltpu
from jax.sharding import PartitionSpec as P

ITERS = 2
SIGMA_PEAK = 4.0
MONITOR_GAIN = 4.0
SHIFT = 4.0
LANES = 128
DEPTH = 4
BASIS = 5
MESH = pl.DeviceIdType.MESH


def stretch(coord, low_width, high_width, total):
    lower_part = jnp.maximum(low_width - coord, 0.0) / low_width
    upper_part = jnp.maximum(coord - (total - 1.0 - high_width), 0.0) / high_width
    damping = SIGMA_PEAK * (
        lower_part * lower_part * lower_part + upper_part * upper_part * upper_part
    )
    denominator = 1.0 + damping * damping
    return (1.0 / denominator, -damping / denominator)


def cmul(a, b):
    return (a[0] * b[0] - a[1] * b[1], a[0] * b[1] + a[1] * b[0])


def cadd(a, b):
    return (a[0] + b[0], a[1] + b[1])


def csub(a, b):
    return (a[0] - b[0], a[1] - b[1])


def cdiv(top, bottom):
    d = bottom[0] * bottom[0] + bottom[1] * bottom[1]
    return (
        (top[0] * bottom[0] + top[1] * bottom[1]) / d,
        (top[1] * bottom[0] - top[0] * bottom[1]) / d,
    )


def three_point(coord, low, high, total):
    below = stretch(coord - 1.0, low, high, total)
    here = stretch(coord, low, high, total)
    above = stretch(coord + 1.0, low, high, total)
    face_low = stretch(coord - 0.5, low, high, total)
    face_high = stretch(coord + 0.5, low, high, total)
    return (
        cmul(face_low, below),
        cmul(cadd(face_low, face_high), here),
        cmul(face_high, above),
    )


def poly_dot(left, right, gram):
    total = None
    for i, a in enumerate(left):
        for j, b in enumerate(right):
            if i <= j:
                g = gram[(i, j)]
            else:
                g = (gram[(j, i)][0], -gram[(j, i)][1])
            term = cmul(cmul((a[0], -a[1]), b), g)
            total = term if total is None else cadd(total, term)
    return total


def poly_energy(q, gram):
    total = None
    for i, a in enumerate(q):
        term = (a[0] * a[0] + a[1] * a[1]) * gram[(i, i)][0]
        total = term if total is None else total + term
        for j in range(i + 1, len(q)):
            b = q[j]
            c_re = a[0] * b[0] + a[1] * b[1]
            c_im = a[0] * b[1] - a[1] * b[0]
            g = gram[(i, j)]
            total = total + 2.0 * (c_re * g[0] - c_im * g[1])
    return total


def poly_scale(c, p):
    return [cmul(c, a) for a in p]


def poly_add(p, q):
    out = []
    for i in range(max(len(p), len(q))):
        if i >= len(p):
            out.append(q[i])
        elif i >= len(q):
            out.append(p[i])
        else:
            out.append(cadd(p[i], q[i]))
    return out


def poly_sub(p, q):
    return poly_add(p, [(-a[0], -a[1]) for a in q])


def poly_image(p):
    raised = [None] + list(p)
    out = []
    for i in range(len(p) + 1):
        if i == 0:
            out.append((SHIFT * p[0][0], SHIFT * p[0][1]))
        elif i == len(p):
            out.append(raised[i])
        else:
            out.append((raised[i][0] + SHIFT * p[i][0], raised[i][1] + SHIFT * p[i][1]))
    return out


def krylov_weights(gram, one, zero):
    unit = (one, zero)
    residual = [unit]
    image = poly_image(residual)
    update = None
    quasi, first_dir, search = residual, residual, image
    direction = None
    start_sq = gram[(0, 0)][0]
    tau = jnp.sqrt(start_sq)
    theta, eta = zero, (zero, zero)
    rho = (start_sq, zero)

    def advance(norm_sq, tau, theta, eta, step, direction, guide, update):
        if direction is None:
            direction = guide
        else:
            ratio = cdiv(eta, step)
            coef = (theta * theta * ratio[0], theta * theta * ratio[1])
            direction = poly_add(guide, poly_scale(coef, direction))
        theta = jnp.sqrt(norm_sq) / tau
        shrink = 1.0 / (1.0 + theta * theta)
        tau = tau * theta * jnp.sqrt(shrink)
        eta = (shrink * step[0], shrink * step[1])
        move = poly_scale(eta, direction)
        update = move if update is None else poly_add(update, move)
        return direction, tau, theta, eta, update

    for iteration in range(ITERS):
        step = cdiv(rho, poly_dot(residual, search, gram))
        quasi = poly_sub(quasi, poly_scale(step, image))
        norm_sq = jnp.maximum(poly_energy(quasi, gram), 0.0)
        direction, tau, theta, eta, update = advance(
            norm_sq, tau, theta, eta, step, direction, first_dir, update
        )
        second_dir = poly_sub(first_dir, poly_scale(step, search))
        second_image = poly_image(second_dir)
        quasi = poly_sub(quasi, poly_scale(step, second_image))
        norm_sq = jnp.maximum(poly_energy(quasi, gram), 0.0)
        direction, tau, theta, eta, update = advance(
            norm_sq, tau, theta, eta, step, direction, second_dir, update
        )
        if iteration + 1 < ITERS:
            rho_new = poly_dot(residual, quasi, gram)
            beta = cdiv(rho_new, rho)
            rho = rho_new
            first_dir = poly_add(quasi, poly_scale(beta, second_dir))
            image = poly_image(first_dir)
            search = poly_add(
                image, poly_scale(beta, poly_add(second_image, poly_scale(beta, search)))
            )
    return update


def kernel(
    n, f_in, s_in, eps_in, wave_in, cell_in, pml_in, owner_in, adj_out, grad_out,
    S, F, V, E, CN, RC, CC, part_out, part_in, tiles, ordered, tiles_in,
    edge_send, edge_recv, sum_send, sum_recv, tile_send, tile_recv,
):
    waves, rows, cols = s_in.shape[1], s_in.shape[2], s_in.shape[3]
    blocks = cols // LANES
    width = cols // n
    me = lax.axis_index("space")
    part = lax.axis_index("parts")
    first = me * rows
    total = rows * n
    up, down = me - 1, me + 1
    has_up, has_down = me > 0, me < n - 1

    barrier = pltpu.get_barrier_semaphore()

    @pl.loop(1, n)
    def _(d):
        pl.semaphore_signal(
            barrier, inc=1, device_id=(part, lax.rem(me + d, n)), device_id_type=MESH
        )

    def at(b):
        return pl.ds(pl.multiple_of(b * LANES, LANES), LANES)

    @pl.loop(0, blocks)
    def _(b):
        for c in range(2):
            S[c, pl.ds(1, rows), :, at(b)] = jnp.swapaxes(s_in[c, :, :, at(b)], 0, 1)

    for r in range(rows):
        E[DEPTH + r] = eps_in[pl.ds(r, 1), :]

    def edge(slot, src, dst, target):
        return pltpu.make_async_remote_copy(
            src_ref=src, dst_ref=dst, send_sem=edge_send.at[slot], recv_sem=edge_recv.at[slot],
            device_id=(part, target), device_id_type=MESH,
        )

    V0 = V.at[0]
    lo, hi = DEPTH, DEPTH + rows
    to_up = [
        edge(0, S.at[:, 1], S.at[:, rows + 1], up),
        edge(1, E.at[pl.ds(lo, DEPTH)], E.at[pl.ds(hi, DEPTH)], up),
        edge(2, V0.at[:, pl.ds(lo + 1, DEPTH - 1)], V0.at[:, pl.ds(hi + 1, DEPTH - 1)], up),
        edge(3, V0.at[:, lo], V0.at[:, hi], up),
    ]
    to_down = [
        edge(4, S.at[:, rows], S.at[:, 0], down),
        edge(5, E.at[pl.ds(hi - DEPTH, DEPTH)], E.at[pl.ds(0, DEPTH)], down),
        edge(6, V0.at[:, pl.ds(hi - DEPTH, DEPTH - 1)], V0.at[:, pl.ds(0, DEPTH - 1)], down),
        edge(7, V0.at[:, hi - 1], V0.at[:, DEPTH - 1], down),
    ]

    def start(i):
        @pl.when(has_up)
        def _():
            to_up[i].start()

        @pl.when(has_down)
        def _():
            to_down[i].start()

    def arrived(i):
        @pl.when(has_up)
        def _():
            to_down[i].wait_recv()

        @pl.when(has_down)
        def _():
            to_up[i].wait_recv()

    def left(i):
        @pl.when(has_up)
        def _():
            to_up[i].wait_send()

        @pl.when(has_down)
        def _():
            to_down[i].wait_send()

    pl.semaphore_wait(barrier, n - 1)
    start(0)
    start(1)

    @pl.when(jnp.logical_not(has_up))
    def _():
        S[:, 0] = jnp.zeros((2, waves, cols), jnp.float32)
        E[pl.ds(0, DEPTH)] = jnp.zeros((DEPTH, 1, cols), jnp.float32)
        V[0, :, pl.ds(0, DEPTH)] = jnp.zeros((2, DEPTH, waves, cols), jnp.float32)

    @pl.when(jnp.logical_not(has_down))
    def _():
        S[:, rows + 1] = jnp.zeros((2, waves, cols), jnp.float32)
        E[pl.ds(hi, DEPTH)] = jnp.zeros((DEPTH, 1, cols), jnp.float32)
        V[0, :, pl.ds(hi, DEPTH)] = jnp.zeros((2, DEPTH, waves, cols), jnp.float32)

    @pl.loop(0, blocks)
    def _(b):
        for c in range(2):
            F[c, :, :, at(b)] = jnp.swapaxes(f_in[c, :, :, at(b)], 0, 1)

    wid = [pml_in[0, i].astype(jnp.float32) for i in range(4)]
    span = rows + 2 * DEPTH
    row_id = lax.broadcasted_iota(jnp.int32, (span, LANES), 0) + (first - DEPTH)
    inside = jnp.logical_and(row_id >= 0, row_id <= total - 1)
    am, a0, ap = three_point(row_id.astype(jnp.float32), wid[0], wid[1], total)
    for i, x in enumerate((am, a0, ap)):
        for c in range(2):
            RC[2 * i + c] = jnp.where(inside, x[c], 0.0)
    RC[2] = jnp.where(inside, a0[0], 0.0) + (2.0 - SHIFT)
    for e, base in enumerate((0, cols - LANES)):
        col_id = (lax.broadcasted_iota(jnp.int32, (8, LANES), 1) + base).astype(jnp.float32)
        bm, b0, bp = three_point(col_id, wid[2], wid[3], cols)
        for i, x in enumerate((bm, b0, bp)):
            for c in range(2):
                CC[e, 2 * i + c] = x[c]
        CC[e, 2] = b0[0] - 2.0

    wave_row = lax.broadcasted_iota(jnp.int32, (waves, LANES), 0)
    k2 = jnp.zeros((waves, LANES), jnp.float32)
    for w in range(waves):
        k2 = jnp.where(wave_row == w, wave_in[0, w], k2)
    k2 = k2 * k2

    m = cell_in.shape[1]
    cells = cell_in[...]
    bits = cols.bit_length() - 1
    cell_rows = lax.shift_right_logical(cells, bits)
    cell_cols = jnp.bitwise_and(cells, cols - 1).astype(jnp.float32)
    rows_hot = (
        cell_rows == lax.broadcasted_iota(jnp.int32, (rows, m), 0) + first
    ).astype(jnp.float32)
    diag = lax.broadcasted_iota(jnp.int32, (m, m), 0) == lax.broadcasted_iota(jnp.int32, (m, m), 1)
    col_at = jnp.sum(
        jnp.where(diag, jnp.broadcast_to(cell_cols, (m, m)), 0.0), axis=1, keepdims=True
    ).astype(jnp.int32)
    cols_hot = (col_at == lax.broadcasted_iota(jnp.int32, (m, cols), 1)).astype(jnp.float32)
    counts = jnp.dot(rows_hot, cols_hot, preferred_element_type=jnp.float32)
    for r in range(rows):
        CN[r] = MONITOR_GAIN * counts[r : r + 1]

    lane = lax.broadcasted_iota(jnp.int32, (waves, LANES), 1)
    is_first, is_last = lane == 0, lane == LANES - 1

    def shifted_image(src, t, r, emit):
        co = [
            jnp.broadcast_to(RC[i, pl.ds(r, 1), :], (waves, LANES)) for i in range(6)
        ]
        rolled = {}

        def get(b):
            if b not in rolled:
                x = [src[c, t, :, pl.ds(b * LANES, LANES)] for c in range(2)]
                rolled[b] = (
                    x,
                    [pltpu.roll(y, 1, 1) for y in x],
                    [pltpu.roll(y, LANES - 1, 1) for y in x],
                )
            return rolled[b]

        for b in range(blocks):
            here = pl.ds(b * LANES, LANES)
            v, r_left, r_right = get(b)
            before = get(b - 1)[1] if b > 0 else (0.0, 0.0)
            after = get(b + 1)[2] if b + 1 < blocks else (0.0, 0.0)
            lf = [jnp.where(is_first, before[c], r_left[c]) for c in range(2)]
            rt = [jnp.where(is_last, after[c], r_right[c]) for c in range(2)]
            above = [src[c, t - 1, :, here] for c in range(2)]
            below = [src[c, t + 1, :, here] for c in range(2)]
            mass = k2 * E[r, :, here]
            d = (co[2] - mass, co[3])
            if b == 0 or b == blocks - 1:
                e = 0 if b == 0 else 1
                cc = [CC[e, i] for i in range(6)]
                d = (d[0] + cc[2], d[1] + cc[3])
                side = cadd(cmul((cc[0], cc[1]), lf), cmul((cc[4], cc[5]), rt))
            else:
                side = cadd(lf, rt)
            out = csub(
                csub(cmul(d, v), side),
                cadd(cmul((co[0], co[1]), above), cmul((co[4], co[5]), below)),
            )
            emit(b, here, v, out)
            rolled.pop(b - 1, None)

    def residual_row(r):
        def emit(b, here, v, out):
            gain = CN[r, :, here]
            V[0, 0, DEPTH + r, :, here] = -gain * F[0, r, :, here] - (out[0] + SHIFT * v[0])
            V[0, 1, DEPTH + r, :, here] = gain * F[1, r, :, here] - (out[1] + SHIFT * v[1])

        shifted_image(S, r + 1, DEPTH + r, emit)

    def raise_row(k, r):
        def emit(b, here, v, out):
            V[k + 1, 0, r, :, here] = out[0]
            V[k + 1, 1, r, :, here] = out[1]

        shifted_image(V.at[k], r, r, emit)

    @pl.loop(1, rows - 1)
    def _(r):
        residual_row(r)

    start(2)
    arrived(0)

    @pl.loop(0, 2)
    def _(i):
        residual_row(i * (rows - 1))

    start(3)
    arrived(1)

    for k in range(DEPTH - 1):
        @pl.loop(lo + 1 + k, hi - 1 - k)
        def _(r):
            raise_row(k, r)

    arrived(2)
    arrived(3)

    for k in range(DEPTH):
        inner_lo, inner_hi = lo + 1 + k, hi - 1 - k
        outer_lo, outer_hi = 1 + k, span - 1 - k
        each = inner_lo - outer_lo
        gap = max(inner_hi - inner_lo, 0)

        @pl.loop(0, 2 * each)
        def _(i):
            raise_row(k, outer_lo + i + (i // each) * gap)

    pairs = [(i, j) for i in range(BASIS) for j in range(i, BASIS)]

    def gram_row(r, acc):
        acc = list(acc)
        for b in range(blocks):
            here = pl.ds(b * LANES, LANES)
            x = [[V[k, c, r, :, here] for c in range(2)] for k in range(BASIS)]
            slot = 0
            for i, j in pairs:
                a, z = x[i], x[j]
                acc[slot] = acc[slot] + (a[0] * z[0] + a[1] * z[1])
                slot += 1
                if i != j:
                    acc[slot] = acc[slot] + (a[0] * z[1] - a[1] * z[0])
                    slot += 1
        return tuple(acc)

    count = BASIS * BASIS
    zero = jnp.zeros((waves, LANES), jnp.float32)
    acc = lax.fori_loop(lo, hi, gram_row, (zero,) * count)
    packed = zero
    for i in range(count):
        packed = jnp.where(lane == i, jnp.sum(acc[i], axis=1, keepdims=True), packed)
    part_out[...] = packed
    part_in[me] = packed

    def sum_copy(d, target):
        return pltpu.make_async_remote_copy(
            src_ref=part_out, dst_ref=part_in.at[me], send_sem=sum_send.at[d],
            recv_sem=sum_recv.at[me], device_id=(part, target), device_id_type=MESH,
        )

    def sum_arrival(source):
        return pltpu.make_async_remote_copy(
            src_ref=part_out, dst_ref=part_in.at[source], send_sem=sum_send.at[0],
            recv_sem=sum_recv.at[source], device_id=(part, source), device_id_type=MESH,
        )

    @pl.loop(1, n)
    def _(d):
        sum_copy(d, lax.rem(me + d, n)).start()

    for i in range(DEPTH):
        left(i)

    @pl.loop(1, n)
    def _(d):
        sum_arrival(lax.rem(me + d, n)).wait_recv()

    @pl.loop(1, n)
    def _(d):
        sum_copy(d, lax.rem(me + d, n)).wait_send()

    whole = part_in[0]
    for i in range(1, n):
        whole = whole + part_in[i]
    gram, slot = {}, 0
    for i, j in pairs:
        re = jnp.broadcast_to(whole[:, slot : slot + 1], (waves, LANES))
        slot += 1
        im = zero
        if i != j:
            im = jnp.broadcast_to(whole[:, slot : slot + 1], (waves, LANES))
            slot += 1
        gram[(i, j)] = (re, im)
    weights = krylov_weights(gram, zero + 1.0, zero)
    k2m = -2.0 * k2

    for b in range(blocks):
        here = pl.ds(b * LANES, LANES)
        sol, grad = ([], []), []
        for r in range(rows):
            x = (S[0, r + 1, :, here], S[1, r + 1, :, here])
            for k, wk in enumerate(weights):
                x = cadd(x, cmul(wk, (V[k, 0, lo + r, :, here], V[k, 1, lo + r, :, here])))
            sol[0].append(x[0])
            sol[1].append(x[1])
            g = k2m * (x[0] * F[0, r, :, here] - x[1] * F[1, r, :, here])
            grad.append(jnp.sum(g, axis=0, keepdims=True))
        for c in range(2):
            adj_out[c, :, :, here] = jnp.swapaxes(jnp.stack(sol[c]), 0, 1)
        tile = jnp.concatenate(grad, axis=0)
        for q in range(LANES // width):
            tiles[b * (LANES // width) + q] = tile[:, q * width : (q + 1) * width]

    @pl.loop(0, n)
    def _(o):
        def pick(k, acc):
            return jnp.where(owner_in[0, k] == o, tiles[k], acc)

        ordered[o] = lax.fori_loop(0, n, pick, jnp.zeros((rows, width), jnp.float32), unroll=True)

    def tile_copy(d, target):
        return pltpu.make_async_remote_copy(
            src_ref=ordered.at[target], dst_ref=tiles_in.at[me], send_sem=tile_send.at[d],
            recv_sem=tile_recv.at[me], device_id=(part, target), device_id_type=MESH,
        )

    def tile_arrival(source):
        return pltpu.make_async_remote_copy(
            src_ref=ordered.at[source], dst_ref=tiles_in.at[source], send_sem=tile_send.at[0],
            recv_sem=tile_recv.at[source], device_id=(part, source), device_id_type=MESH,
        )

    @pl.loop(1, n)
    def _(d):
        tile_copy(d, lax.rem(me + d, n)).start()

    tiles_in[me] = ordered[me]

    @pl.loop(1, n)
    def _(d):
        tile_arrival(lax.rem(me + d, n)).wait_recv()

    @pl.loop(1, n)
    def _(d):
        tile_copy(d, lax.rem(me + d, n)).wait_send()

    for r in range(rows):
        grad_out[0, :, r * width : (r + 1) * width] = tiles_in[:, r, :]


def local(
    forward_field, adjoint_start, permittivity, wavenumbers, monitor_cells, pml_widths, owner_map
):
    n = lax.axis_size("space")
    _, waves, rows, cols = adjoint_start.shape
    width = cols // n
    span = rows + 2 * DEPTH
    f32 = jnp.float32
    vmem = pl.BlockSpec(memory_space=pltpu.VMEM)
    smem = pl.BlockSpec(memory_space=pltpu.SMEM)
    dma = pltpu.SemaphoreType.DMA
    return pl.pallas_call(
        functools.partial(kernel, n),
        out_shape=(
            jax.ShapeDtypeStruct(adjoint_start.shape, f32),
            jax.ShapeDtypeStruct((1, n, rows * width), f32),
        ),
        in_specs=[vmem, vmem, vmem, smem, vmem, smem, smem],
        out_specs=(vmem, vmem),
        scratch_shapes=[
            pltpu.VMEM((2, rows + 2, waves, cols), f32),
            pltpu.VMEM((2, rows, waves, cols), f32),
            pltpu.VMEM((BASIS, 2, span, waves, cols), f32),
            pltpu.VMEM((span, 1, cols), f32),
            pltpu.VMEM((rows, 1, cols), f32),
            pltpu.VMEM((6, span, LANES), f32),
            pltpu.VMEM((2, 6, 8, LANES), f32),
            pltpu.VMEM((waves, LANES), f32),
            pltpu.VMEM((n, waves, LANES), f32),
            pltpu.VMEM((n, rows, width), f32),
            pltpu.VMEM((n, rows, width), f32),
            pltpu.VMEM((n, rows, width), f32),
            dma((8,)),
            dma((8,)),
            dma((n,)),
            dma((n,)),
            dma((n,)),
            dma((n,)),
        ],
        compiler_params=pltpu.CompilerParams(
            collective_id=0, has_side_effects=True, vmem_limit_bytes=40 * 1024 * 1024
        ),
    )(
        forward_field,
        adjoint_start,
        permittivity,
        wavenumbers.reshape(1, -1),
        monitor_cells.reshape(1, -1),
        pml_widths.reshape(1, -1),
        owner_map,
    )


def solution(mesh):
    placed = (
        P(None, "parts", "space", None),
        P(None, "parts", "space", None),
        P(("parts", "space"), None),
        P("parts"),
        P("parts"),
        P("parts"),
        P(("parts", "space"), None),
    )
    return jax.shard_map(
        local,
        mesh=mesh,
        in_specs=placed,
        out_specs=(P(None, "parts", "space", None), P(("parts", "space"), None, None)),
        check_vma=False,
    )
```

time: 209 us -> 47.8 us (0.23)
  blocking collectives: 135 us -> 0 us
  Pallas kernels: 0 us -> 41.4 us
  other arithmetic: 30.4 us -> 0 us
  starting transfers between devices: 23.9 us -> 0 us
  local copies, waits for them, and re-layouts: 12.7 us -> 5.56 us
  between operations: 2.97 us -> 0.68 us
  waiting for transfers between devices: 2.17 us -> 0 us
    psum x4 -> x0, blocking collectives: 126 us -> none  [the longest x1 34.1 us: local(): start_sq = lax.psum(energy(residual), 'space')]
    pallas_call x0 -> x1, Pallas kernels: none -> 41.4 us  [local(): pl.pallas_call(functools.partial(kernel, n), out_shape=(jax.ShapeDtypeStr...]
    ppermute x10 -> x0, starting transfers between devices: 23.9 us -> none  [the longest x5 17.5 us: with_halo(): lax.ppermute(tail, axis, [(i, (i + 1) % count) for i in range(ends)])]
    sub x20 -> x0, other arithmetic: 9.72 us -> none  [the longest x7 4.09 us: times_field(): c_re * field[0] - c_im * field[1]]
    all_to_all x1 -> x0, blocking collectives: 9.48 us -> none  [local(): lax.all_to_all(ordered, 'space', split_axis=0, concat_axis=0, tiled=True)]
    div x11 -> x0, other arithmetic: 5.28 us -> none  [the longest x6 5.18 us: stretch(): return (1.0 / denominator, -damping / denominator)]
    add x20 -> x0, other arithmetic: 4.94 us -> none  [the longest x5 1.75 us: operate(): q_im = cen_re[:, None] * padded[1] + cen_im[:, None] * padded[0]]
    another operation x13 -> x0, other arithmetic: 3.89 us -> none  [the longest x6 3.33 us: times_field(): jnp.stack([c_re * field[0] - c_im * field[1], c_re * field[1] + c_im * fi...]
  transfers between devices with their start and end apart: 10 -> 0, of which waited for: 4 -> 0; matrix products, arithmetic and copies ran while one was open for 5% -> 0% of each run, Pallas kernels for 0% -> 0%
where the time goes in v1:
time: 47.8 us; the launch traced here: 47.6 us
  Pallas kernels  41.4 us (87%)
  local copies, waits for them, and re-layouts  5.56 us (12%)
  between operations  0.68 us (1%)
    pallas_call x1, Pallas kernels, local(): pl.pallas_call(functools.partial(kernel, n), out_shape=(jax.ShapeDtypeStr...  41.4 us
    unnamed x16, local copies, waits for them, and re-layouts  5.56 us

profile of v1, /device:TPU:0, one launch (start us, length us, event | category | flops | bytes accessed | tf_op | source)
XLA Modules:
  0.0 47.6 jit_solution(18230960218969806222)
XLA Ops:
  0.6 0.0 copy-start.6
  0.6 0.0 copy-start.3
  0.7 0.0 copy-start.4
  0.7 0.0 copy-start.5
  0.7 0.6 %copy-done.6 = s32[1,16]{1,0:T(1,128)S(1)} copy-done((s32[1,16]{1,0:T(1,128)S(1)}, s32[1,16]{1,0:T(1,128)}, u32[]{:S(2)}) %copy-start.6) | copy-done | bytes 88
  1.3 0.0 copy-done.3
  1.3 0.0 copy-done.4
  1.3 0.0 copy-done.5
  1.3 0.0 copy-start
  1.3 1.2 %copy-done = f32[2,8,8,2048]{3,2,1,0:T(8,128)S(1)} copy-done((f32[2,8,8,2048]{3,2,1,0:T(8,128)S(1)}, f32[2,8,8,2048]{3,2,1,0:T(8,128)}, u32[]{:S(2)}) %copy-start) | copy-done | bytes 1048600
  2.6 0.0 copy-start.1
  2.6 1.2 %copy-done.1 = f32[2,8,8,2048]{3,2,1,0:T(8,128)S(1)} copy-done((f32[2,8,8,2048]{3,2,1,0:T(8,128)S(1)}, f32[2,8,8,2048]{3,2,1,0:T(8,128)}, u32[]{:S(2)}) %copy-start.1) | copy-done | bytes 1048600
  3.8 0.0 copy-start.2
  3.8 0.8 %copy-done.2 = f32[8,2048]{1,0:T(8,128)S(1)} copy-done((f32[8,2048]{1,0:T(8,128)S(1)}, f32[8,2048]{1,0:T(8,128)}, u32[]{:S(2)}) %copy-start.2) | copy-done | bytes 65560
  4.6 41.4 %shard_map.86 = (f32[2,8,8,2048]{3,2,1,0:T(8,128)S(1)}, f32[1,16,1024]{2,1,0:T(8,128)S(1)}) custom-call(f32[2,8,8,2048]{3,2,1,0:T(8,128)S(1)} %copy-done, f32[2,8,8,2048]{3,2,1,0:T(8,128)S(1)} %copy-done.1, f32[8,2048]{1,0:T(8,128)S(1)} %copy-done.2, f32[1,8]{1,0:T(1,128)S(1)} %bitcast.3, s32[1,64]{1,0:T(1,128)S(1)} %bitcast.4, s32[1,4]{1,0:T(1,128)S(1)} %bitcast.5, ...), custom_call_target="tpu_custom_call" | custom-call | tf_op jit(solution)/shard_map/pallas_call | solution.py:543
  46.0 1.0 %copy.11 = f32[2,8,8,2048]{3,2,1,0:T(8,128)} copy(f32[2,8,8,2048]{3,2,1,0:T(8,128)S(1)} %get-tuple-element.4) | data formatting | bytes 2097152
  47.0 0.6 %copy.12 = f32[1,16,1024]{2,1,0:T(8,128)} copy(f32[1,16,1024]{2,1,0:T(8,128)S(1)} %get-tuple-element.5) | data formatting | bytes 131072
Async XLA Ops:
  0.6 0.7 %copy-start.6 = (s32[1,16]{1,0:T(1,128)S(1)}, s32[1,16]{1,0:T(1,128)}, u32[]{:S(2)}) copy-start(s32[1,16]{1,0:T(1,128)} %owner_in.1) | copy-start | bytes 196
  0.6 0.7 %copy-start.3 = (f32[8]{0:T(128)S(1)}, f32[8]{0:T(128)}, u32[]{:S(2)}) copy-start(f32[8]{0:T(128)} %param.10) | copy-start | bytes 100
  0.7 0.7 %copy-start.4 = (s32[64]{0:T(128)S(1)}, s32[64]{0:T(128)}, u32[]{:S(2)}) copy-start(s32[64]{0:T(128)} %param.11) | copy-start | bytes 772
  0.7 0.7 %copy-start.5 = (s32[4]{0:T(128)S(1)}, s32[4]{0:T(128)}, u32[]{:S(2)}) copy-start(s32[4]{0:T(128)} %param.12) | copy-start | bytes 52
  1.3 1.2 %copy-start = (f32[2,8,8,2048]{3,2,1,0:T(8,128)S(1)}, f32[2,8,8,2048]{3,2,1,0:T(8,128)}, u32[]{:S(2)}) copy-start(f32[2,8,8,2048]{3,2,1,0:T(8,128)} %f_in.1) | copy-start | bytes 3145732
  2.6 1.2 %copy-start.1 = (f32[2,8,8,2048]{3,2,1,0:T(8,128)S(1)}, f32[2,8,8,2048]{3,2,1,0:T(8,128)}, u32[]{:S(2)}) copy-start(f32[2,8,8,2048]{3,2,1,0:T(8,128)} %s_in.1) | copy-start | bytes 3145732
  3.8 0.8 %copy-start.2 = (f32[8,2048]{1,0:T(8,128)S(1)}, f32[8,2048]{1,0:T(8,128)}, u32[]{:S(2)}) copy-start(f32[8,2048]{1,0:T(8,128)} %eps_in.1) | copy-start | bytes 196612

commit v2 on v1

--- a/solution.py
+++ b/solution.py
@@ -174,9 +174,9 @@
 
 
 def kernel(
-    n, f_in, s_in, eps_in, wave_in, cell_in, pml_in, owner_in, adj_out, grad_out,
-    S, F, V, E, CN, RC, CC, part_out, part_in, tiles, ordered, tiles_in,
-    edge_send, edge_recv, sum_send, sum_recv, tile_send, tile_recv,
+    n, f_hbm, s_hbm, eps_hbm, wave_in, cell_in, pml_in, owner_in, adj_out, grad_out,
+    f_in, s_in, eps_in, S, F, V, E, CN, RC, CC, part_out, part_in, tiles, ordered, tiles_in,
+    tile_of, load_sem, edge_send, edge_recv, sum_send, sum_recv, tile_send, tile_recv,
 ):
     waves, rows, cols = s_in.shape[1], s_in.shape[2], s_in.shape[3]
     blocks = cols // LANES
@@ -188,6 +188,14 @@
     up, down = me - 1, me + 1
     has_up, has_down = me > 0, me < n - 1
 
+    load_f = pltpu.make_async_copy(f_hbm, f_in, load_sem.at[0])
+    load_eps = pltpu.make_async_copy(eps_hbm, eps_in, load_sem.at[1])
+    load_s = [pltpu.make_async_copy(s_hbm.at[c], s_in.at[c], load_sem.at[2 + c]) for c in range(2)]
+    load_s[0].start()
+    load_s[1].start()
+    load_eps.start()
+    load_f.start()
+
     barrier = pltpu.get_barrier_semaphore()
 
     @pl.loop(1, n)
@@ -199,13 +207,12 @@
     def at(b):
         return pl.ds(pl.multiple_of(b * LANES, LANES), LANES)
 
-    @pl.loop(0, blocks)
-    def _(b):
-        for c in range(2):
+    for c in range(2):
+        load_s[c].wait()
+
+        @pl.loop(0, blocks)
+        def _(b):
             S[c, pl.ds(1, rows), :, at(b)] = jnp.swapaxes(s_in[c, :, :, at(b)], 0, 1)
-
-    for r in range(rows):
-        E[DEPTH + r] = eps_in[pl.ds(r, 1), :]
 
     def edge(slot, src, dst, target):
         return pltpu.make_async_remote_copy(
@@ -215,49 +222,54 @@
 
     V0 = V.at[0]
     lo, hi = DEPTH, DEPTH + rows
-    to_up = [
-        edge(0, S.at[:, 1], S.at[:, rows + 1], up),
-        edge(1, E.at[pl.ds(lo, DEPTH)], E.at[pl.ds(hi, DEPTH)], up),
-        edge(2, V0.at[:, pl.ds(lo + 1, DEPTH - 1)], V0.at[:, pl.ds(hi + 1, DEPTH - 1)], up),
-        edge(3, V0.at[:, lo], V0.at[:, hi], up),
-    ]
-    to_down = [
-        edge(4, S.at[:, rows], S.at[:, 0], down),
-        edge(5, E.at[pl.ds(hi - DEPTH, DEPTH)], E.at[pl.ds(0, DEPTH)], down),
-        edge(6, V0.at[:, pl.ds(hi - DEPTH, DEPTH - 1)], V0.at[:, pl.ds(0, DEPTH - 1)], down),
-        edge(7, V0.at[:, hi - 1], V0.at[:, DEPTH - 1], down),
-    ]
+    reach = DEPTH - 1
+    slots = DEPTH + 2
+
+    def to_up(i):
+        if isinstance(i, int) and i == 0:
+            return edge(0, S.at[:, 1], S.at[:, rows + 1], up)
+        if isinstance(i, int) and i == 1:
+            return edge(1, E.at[pl.ds(lo, reach)], E.at[pl.ds(hi, reach)], up)
+        return edge(i, V0.at[:, lo + i - 2], V0.at[:, hi + i - 2], up)
+
+    def to_down(i):
+        if isinstance(i, int) and i == 0:
+            return edge(slots, S.at[:, rows], S.at[:, 0], down)
+        if isinstance(i, int) and i == 1:
+            return edge(
+                slots + 1, E.at[pl.ds(hi - reach, reach)], E.at[pl.ds(lo - reach, reach)], down
+            )
+        return edge(slots + i, V0.at[:, hi + 1 - i], V0.at[:, lo + 1 - i], down)
 
     def start(i):
         @pl.when(has_up)
         def _():
-            to_up[i].start()
+            to_up(i).start()
 
         @pl.when(has_down)
         def _():
-            to_down[i].start()
+            to_down(i).start()
 
     def arrived(i):
         @pl.when(has_up)
         def _():
-            to_down[i].wait_recv()
+            to_down(i).wait_recv()
 
         @pl.when(has_down)
         def _():
-            to_up[i].wait_recv()
+            to_up(i).wait_recv()
 
     def left(i):
         @pl.when(has_up)
         def _():
-            to_up[i].wait_send()
+            to_up(i).wait_send()
 
         @pl.when(has_down)
         def _():
-            to_down[i].wait_send()
+            to_down(i).wait_send()
 
     pl.semaphore_wait(barrier, n - 1)
     start(0)
-    start(1)
 
     @pl.when(jnp.logical_not(has_up))
     def _():
@@ -270,6 +282,13 @@
         S[:, rows + 1] = jnp.zeros((2, waves, cols), jnp.float32)
         E[pl.ds(hi, DEPTH)] = jnp.zeros((DEPTH, 1, cols), jnp.float32)
         V[0, :, pl.ds(hi, DEPTH)] = jnp.zeros((2, DEPTH, waves, cols), jnp.float32)
+
+    load_eps.wait()
+    for r in range(rows):
+        E[DEPTH + r] = eps_in[pl.ds(r, 1), :]
+    start(1)
+
+    load_f.wait()
 
     @pl.loop(0, blocks)
     def _(b):
@@ -375,37 +394,39 @@
 
         shifted_image(V.at[k], r, r, emit)
 
-    @pl.loop(1, rows - 1)
+    @pl.loop(0, 2)
+    def _(i):
+        residual_row(1 + i * (rows - 3))
+
+    start(3)
+
+    @pl.loop(2, rows - 2)
     def _(r):
         residual_row(r)
 
-    start(2)
     arrived(0)
 
     @pl.loop(0, 2)
     def _(i):
         residual_row(i * (rows - 1))
 
-    start(3)
-    arrived(1)
+    start(2)
+    start(4)
+    start(5)
+
+    @pl.loop(0, n)
+    def _(o):
+        def count(k, found):
+            return jnp.where(owner_in[0, k] == o, k, found)
+
+        tile_of[o] = lax.fori_loop(0, n, count, jnp.int32(0), unroll=True)
 
     for k in range(DEPTH - 1):
         @pl.loop(lo + 1 + k, hi - 1 - k)
         def _(r):
             raise_row(k, r)
 
-    arrived(2)
-    arrived(3)
-
-    for k in range(DEPTH):
-        inner_lo, inner_hi = lo + 1 + k, hi - 1 - k
-        outer_lo, outer_hi = 1 + k, span - 1 - k
-        each = inner_lo - outer_lo
-        gap = max(inner_hi - inner_lo, 0)
-
-        @pl.loop(0, 2 * each)
-        def _(i):
-            raise_row(k, outer_lo + i + (i // each) * gap)
+    arrived(1)
 
     pairs = [(i, j) for i in range(BASIS) for j in range(i, BASIS)]
 
@@ -426,12 +447,35 @@
 
     count = BASIS * BASIS
     zero = jnp.zeros((waves, LANES), jnp.float32)
-    acc = lax.fori_loop(lo, hi, gram_row, (zero,) * count)
+
+    def stage(j, acc):
+        arrived(1 + j)
+
+        @pl.loop(0, 2 * DEPTH)
+        def _(i):
+            k = i // 2
+            d = j - 1 - k
+            raise_row(k, lo - d + lax.rem(i, 2) * (rows - 1 + 2 * d))
+
+        def near(i, acc):
+            d = DEPTH - j
+            return gram_row(lo + d + i * (rows - 1 - 2 * d), acc)
+
+        return lax.fori_loop(0, 2, near, acc)
+
+    acc = lax.fori_loop(1, DEPTH + 1, stage, (zero,) * count)
     packed = zero
     for i in range(count):
         packed = jnp.where(lane == i, jnp.sum(acc[i], axis=1, keepdims=True), packed)
-    part_out[...] = packed
-    part_in[me] = packed
+    group = LANES // 32
+    spread = zero
+    for g in range(group):
+        moved = packed if g == 0 else pltpu.roll(packed, 32 * g, 1)
+        spread = jnp.where(lax.rem(wave_row, group) == g, moved, spread)
+    for q in range(waves // group):
+        mine = jnp.logical_and(wave_row >= q * group, wave_row < (q + 1) * group)
+        part_out[q : q + 1, :] = jnp.sum(jnp.where(mine, spread, 0.0), axis=0, keepdims=True)
+    part_in[me] = part_out[...]
 
     def sum_copy(d, target):
         return pltpu.make_async_remote_copy(
@@ -449,20 +493,21 @@
     def _(d):
         sum_copy(d, lax.rem(me + d, n)).start()
 
-    for i in range(DEPTH):
+    for i in range(slots):
         left(i)
 
     @pl.loop(1, n)
     def _(d):
         sum_arrival(lax.rem(me + d, n)).wait_recv()
 
-    @pl.loop(1, n)
-    def _(d):
-        sum_copy(d, lax.rem(me + d, n)).wait_send()
-
-    whole = part_in[0]
+    summed = part_in[0]
     for i in range(1, n):
-        whole = whole + part_in[i]
+        summed = summed + part_in[i]
+    whole = zero
+    for w in range(waves):
+        row = jnp.broadcast_to(summed[w // group : w // group + 1, :], (waves, LANES))
+        back = (LANES - 32 * (w % group)) % LANES
+        whole = jnp.where(wave_row == w, pltpu.roll(row, back, 1) if back else row, whole)
     gram, slot = {}, 0
     for i, j in pairs:
         re = jnp.broadcast_to(whole[:, slot : slot + 1], (waves, LANES))
@@ -477,27 +522,21 @@
 
     for b in range(blocks):
         here = pl.ds(b * LANES, LANES)
-        sol, grad = ([], []), []
+        grad = []
         for r in range(rows):
             x = (S[0, r + 1, :, here], S[1, r + 1, :, here])
             for k, wk in enumerate(weights):
                 x = cadd(x, cmul(wk, (V[k, 0, lo + r, :, here], V[k, 1, lo + r, :, here])))
-            sol[0].append(x[0])
-            sol[1].append(x[1])
+            V[0, 0, lo + r, :, here] = x[0]
+            V[0, 1, lo + r, :, here] = x[1]
             g = k2m * (x[0] * F[0, r, :, here] - x[1] * F[1, r, :, here])
             grad.append(jnp.sum(g, axis=0, keepdims=True))
-        for c in range(2):
-            adj_out[c, :, :, here] = jnp.swapaxes(jnp.stack(sol[c]), 0, 1)
         tile = jnp.concatenate(grad, axis=0)
         for q in range(LANES // width):
             tiles[b * (LANES // width) + q] = tile[:, q * width : (q + 1) * width]
 
-    @pl.loop(0, n)
-    def _(o):
-        def pick(k, acc):
-            return jnp.where(owner_in[0, k] == o, tiles[k], acc)
-
-        ordered[o] = lax.fori_loop(0, n, pick, jnp.zeros((rows, width), jnp.float32), unroll=True)
+    for o in range(n):
+        ordered[o] = tiles[tile_of[o]]
 
     def tile_copy(d, target):
         return pltpu.make_async_remote_copy(
@@ -516,6 +555,15 @@
         tile_copy(d, lax.rem(me + d, n)).start()
 
     tiles_in[me] = ordered[me]
+
+    @pl.loop(0, blocks)
+    def _(b):
+        for c in range(2):
+            adj_out[c, :, :, at(b)] = jnp.swapaxes(V[0, c, pl.ds(lo, rows), :, at(b)], 0, 1)
+
+    @pl.loop(1, n)
+    def _(d):
+        sum_copy(d, lax.rem(me + d, n)).wait_send()
 
     @pl.loop(1, n)
     def _(d):
@@ -539,6 +587,7 @@
     f32 = jnp.float32
     vmem = pl.BlockSpec(memory_space=pltpu.VMEM)
     smem = pl.BlockSpec(memory_space=pltpu.SMEM)
+    hbm = pl.BlockSpec(memory_space=pltpu.HBM)
     dma = pltpu.SemaphoreType.DMA
     return pl.pallas_call(
         functools.partial(kernel, n),
@@ -546,9 +595,12 @@
             jax.ShapeDtypeStruct(adjoint_start.shape, f32),
             jax.ShapeDtypeStruct((1, n, rows * width), f32),
         ),
-        in_specs=[vmem, vmem, vmem, smem, vmem, smem, smem],
+        in_specs=[hbm, hbm, hbm, smem, vmem, smem, smem],
         out_specs=(vmem, vmem),
         scratch_shapes=[
+            pltpu.VMEM((2, waves, rows, cols), f32),
+            pltpu.VMEM((2, waves, rows, cols), f32),
+            pltpu.VMEM((rows, cols), f32),
             pltpu.VMEM((2, rows + 2, waves, cols), f32),
             pltpu.VMEM((2, rows, waves, cols), f32),
             pltpu.VMEM((BASIS, 2, span, waves, cols), f32),
@@ -556,13 +608,15 @@
             pltpu.VMEM((rows, 1, cols), f32),
             pltpu.VMEM((6, span, LANES), f32),
             pltpu.VMEM((2, 6, 8, LANES), f32),
-            pltpu.VMEM((waves, LANES), f32),
-            pltpu.VMEM((n, waves, LANES), f32),
+            pltpu.VMEM((waves * 32 // LANES, LANES), f32),
+            pltpu.VMEM((n, waves * 32 // LANES, LANES), f32),
             pltpu.VMEM((n, rows, width), f32),
             pltpu.VMEM((n, rows, width), f32),
             pltpu.VMEM((n, rows, width), f32),
-            dma((8,)),
-            dma((8,)),
+            pltpu.SMEM((n,), jnp.int32),
+            dma((4,)),
+            dma((2 * DEPTH + 4,)),
+            dma((2 * DEPTH + 4,)),
             dma((n,)),
             dma((n,)),
             dma((n,)),

time: 47.8 us -> 74.2 us (1.55)
  Pallas kernels: 41.4 us -> 67.7 us
    pallas_call x1, Pallas kernels: 41.4 us -> 67.7 us  [local(): pl.pallas_call(functools.partial(kernel, n), out_shape=(jax.ShapeDtypeStr...]
where the time goes in v2:
time: 74.2 us; the launch traced here: 73.9 us
  Pallas kernels  67.7 us (91%)
  local copies, waits for them, and re-layouts  5.56 us (7%)
    pallas_call x1, Pallas kernels, local(): pl.pallas_call(functools.partial(kernel, n), out_shape=(jax.ShapeDtypeStr...  67.7 us
    unnamed x16, local copies, waits for them, and re-layouts  5.56 us

profile of v2, /device:TPU:0, one launch (start us, length us, event | category | flops | bytes accessed | tf_op | source)
XLA Modules:
  0.0 73.9 jit_solution(434817782619263293)
XLA Ops:
  0.6 0.0 copy-start.6
  0.6 0.0 copy-start.3
  0.7 0.0 copy-start.4
  0.7 0.0 copy-start.5
  0.7 0.6 copy-done.6
  1.3 0.0 copy-done.3
  1.3 0.0 copy-done.4
  1.3 0.0 copy-done.5
  1.3 0.0 copy-start
  1.3 1.2 %copy-done = f32[2,8,8,2048]{3,2,1,0:T(8,128)S(1)} copy-done((f32[2,8,8,2048]{3,2,1,0:T(8,128)S(1)}, f32[2,8,8,2048]{3,2,1,0:T(8,128)}, u32[]{:S(2)}) %copy-start) | copy-done | bytes 1048600
  2.6 0.0 copy-start.1
  2.6 1.2 %copy-done.1 = f32[2,8,8,2048]{3,2,1,0:T(8,128)S(1)} copy-done((f32[2,8,8,2048]{3,2,1,0:T(8,128)S(1)}, f32[2,8,8,2048]{3,2,1,0:T(8,128)}, u32[]{:S(2)}) %copy-start.1) | copy-done | bytes 1048600
  3.8 0.0 copy-start.2
  3.8 0.8 %copy-done.2 = f32[8,2048]{1,0:T(8,128)S(1)} copy-done((f32[8,2048]{1,0:T(8,128)S(1)}, f32[8,2048]{1,0:T(8,128)}, u32[]{:S(2)}) %copy-start.2) | copy-done | bytes 65560
  4.6 67.7 %shard_map.86 = (f32[2,8,8,2048]{3,2,1,0:T(8,128)S(1)}, f32[1,16,1024]{2,1,0:T(8,128)S(1)}) custom-call(f32[2,8,8,2048]{3,2,1,0:T(8,128)S(1)} %copy-done, f32[2,8,8,2048]{3,2,1,0:T(8,128)S(1)} %copy-done.1, f32[8,2048]{1,0:T(8,128)S(1)} %copy-done.2, f32[1,8]{1,0:T(1,128)S(1)} %bitcast.3, s32[1,64]{1,0:T(1,128)S(1)} %bitcast.4, s32[1,4]{1,0:T(1,128)S(1)} %bitcast.5, ...), custom_call_target="tpu_custom_call" | custom-call | tf_op jit(solution)/shard_map/pallas_call | solution.py:592
  72.3 1.0 %copy.11 = f32[2,8,8,2048]{3,2,1,0:T(8,128)} copy(f32[2,8,8,2048]{3,2,1,0:T(8,128)S(1)} %get-tuple-element.4) | data formatting | bytes 2097152
  73.3 0.6 copy.12
Async XLA Ops:
  0.6 0.7 copy-start.6
  0.6 0.7 copy-start.3
  0.7 0.7 copy-start.4
  0.7 0.7 copy-start.5
  1.3 1.2 %copy-start = (f32[2,8,8,2048]{3,2,1,0:T(8,128)S(1)}, f32[2,8,8,2048]{3,2,1,0:T(8,128)}, u32[]{:S(2)}) copy-start(f32[2,8,8,2048]{3,2,1,0:T(8,128)} %f_hbm.1) | copy-start | bytes 3145732
  2.6 1.2 %copy-start.1 = (f32[2,8,8,2048]{3,2,1,0:T(8,128)S(1)}, f32[2,8,8,2048]{3,2,1,0:T(8,128)}, u32[]{:S(2)}) copy-start(f32[2,8,8,2048]{3,2,1,0:T(8,128)} %s_hbm.1) | copy-start | bytes 3145732
  3.8 0.8 %copy-start.2 = (f32[8,2048]{1,0:T(8,128)S(1)}, f32[8,2048]{1,0:T(8,128)}, u32[]{:S(2)}) copy-start(f32[8,2048]{1,0:T(8,128)} %eps_hbm.1) | copy-start | bytes 196612

commit v3 on v2

--- a/solution.py
+++ b/solution.py
@@ -398,12 +398,11 @@
     def _(i):
         residual_row(1 + i * (rows - 3))
 
-    start(3)
-
     @pl.loop(2, rows - 2)
     def _(r):
         residual_row(r)
 
+    left(0)
     arrived(0)
 
     @pl.loop(0, 2)
@@ -411,8 +410,7 @@
         residual_row(i * (rows - 1))
 
     start(2)
-    start(4)
-    start(5)
+    start(3)
 
     @pl.loop(0, n)
     def _(o):
@@ -426,6 +424,9 @@
         def _(r):
             raise_row(k, r)
 
+    left(2)
+    start(4)
+    left(3)
     arrived(1)
 
     pairs = [(i, j) for i in range(BASIS) for j in range(i, BASIS)]
@@ -451,11 +452,12 @@
     def stage(j, acc):
         arrived(1 + j)
 
-        @pl.loop(0, 2 * DEPTH)
-        def _(i):
-            k = i // 2
+        for k in range(DEPTH):
             d = j - 1 - k
-            raise_row(k, lo - d + lax.rem(i, 2) * (rows - 1 + 2 * d))
+
+            @pl.loop(0, 2)
+            def _(i):
+                raise_row(k, lo - d + i * (rows - 1 + 2 * d))
 
         def near(i, acc):
             d = DEPTH - j
@@ -463,7 +465,10 @@
 
         return lax.fori_loop(0, 2, near, acc)
 
-    acc = lax.fori_loop(1, DEPTH + 1, stage, (zero,) * count)
+    acc = lax.fori_loop(1, 2, stage, (zero,) * count)
+    left(4)
+    start(5)
+    acc = lax.fori_loop(2, DEPTH + 1, stage, acc)
     packed = zero
     for i in range(count):
         packed = jnp.where(lane == i, jnp.sum(acc[i], axis=1, keepdims=True), packed)
@@ -493,8 +498,8 @@
     def _(d):
         sum_copy(d, lax.rem(me + d, n)).start()
 
-    for i in range(slots):
-        left(i)
+    left(1)
+    left(5)
 
     @pl.loop(1, n)
     def _(d):

time: 74.2 us -> 43.6 us (0.59)
  Pallas kernels: 67.7 us -> 37.2 us
    pallas_call x1, Pallas kernels: 67.7 us -> 37.2 us  [local(): pl.pallas_call(functools.partial(kernel, n), out_shape=(jax.ShapeDtypeStr...]
where the time goes in v3:
time: 43.6 us; the launch traced here: 43.4 us
  Pallas kernels  37.2 us (85%)
  local copies, waits for them, and re-layouts  5.56 us (13%)
  between operations  0.68 us (2%)
    pallas_call x1, Pallas kernels, local(): pl.pallas_call(functools.partial(kernel, n), out_shape=(jax.ShapeDtypeStr...  37.2 us
    unnamed x16, local copies, waits for them, and re-layouts  5.56 us

profile of v3, /device:TPU:0, one launch (start us, length us, event | category | flops | bytes accessed | tf_op | source)
XLA Modules:
  0.0 43.4 jit_solution(7749171573120357605)
XLA Ops:
  0.6 0.0 copy-start.6
  0.6 0.0 copy-start.3
  0.7 0.0 copy-start.4
  0.7 0.0 copy-start.5
  0.7 0.6 %copy-done.6 = s32[1,16]{1,0:T(1,128)S(1)} copy-done((s32[1,16]{1,0:T(1,128)S(1)}, s32[1,16]{1,0:T(1,128)}, u32[]{:S(2)}) %copy-start.6) | copy-done | bytes 88
  1.3 0.0 copy-done.3
  1.3 0.0 copy-done.4
  1.3 0.0 copy-done.5
  1.3 0.0 copy-start
  1.3 1.2 %copy-done = f32[2,8,8,2048]{3,2,1,0:T(8,128)S(1)} copy-done((f32[2,8,8,2048]{3,2,1,0:T(8,128)S(1)}, f32[2,8,8,2048]{3,2,1,0:T(8,128)}, u32[]{:S(2)}) %copy-start) | copy-done | bytes 1048600
  2.6 0.0 copy-start.1
  2.6 1.2 %copy-done.1 = f32[2,8,8,2048]{3,2,1,0:T(8,128)S(1)} copy-done((f32[2,8,8,2048]{3,2,1,0:T(8,128)S(1)}, f32[2,8,8,2048]{3,2,1,0:T(8,128)}, u32[]{:S(2)}) %copy-start.1) | copy-done | bytes 1048600
  3.8 0.0 copy-start.2
  3.8 0.8 %copy-done.2 = f32[8,2048]{1,0:T(8,128)S(1)} copy-done((f32[8,2048]{1,0:T(8,128)S(1)}, f32[8,2048]{1,0:T(8,128)}, u32[]{:S(2)}) %copy-start.2) | copy-done | bytes 65560
  4.6 37.2 %shard_map.86 = (f32[2,8,8,2048]{3,2,1,0:T(8,128)S(1)}, f32[1,16,1024]{2,1,0:T(8,128)S(1)}) custom-call(f32[2,8,8,2048]{3,2,1,0:T(8,128)S(1)} %copy-done, f32[2,8,8,2048]{3,2,1,0:T(8,128)S(1)} %copy-done.1, f32[8,2048]{1,0:T(8,128)S(1)} %copy-done.2, f32[1,8]{1,0:T(1,128)S(1)} %bitcast.3, s32[1,64]{1,0:T(1,128)S(1)} %bitcast.4, s32[1,4]{1,0:T(1,128)S(1)} %bitcast.5, ...), custom_call_target="tpu_custom_call" | custom-call | tf_op jit(solution)/shard_map/pallas_call | solution.py:597
  41.8 1.0 %copy.11 = f32[2,8,8,2048]{3,2,1,0:T(8,128)} copy(f32[2,8,8,2048]{3,2,1,0:T(8,128)S(1)} %get-tuple-element.4) | data formatting | bytes 2097152
  42.8 0.6 %copy.12 = f32[1,16,1024]{2,1,0:T(8,128)} copy(f32[1,16,1024]{2,1,0:T(8,128)S(1)} %get-tuple-element.5) | data formatting | bytes 131072
Async XLA Ops:
  0.6 0.7 %copy-start.6 = (s32[1,16]{1,0:T(1,128)S(1)}, s32[1,16]{1,0:T(1,128)}, u32[]{:S(2)}) copy-start(s32[1,16]{1,0:T(1,128)} %owner_in.1) | copy-start | bytes 196
  0.6 0.7 %copy-start.3 = (f32[8]{0:T(128)S(1)}, f32[8]{0:T(128)}, u32[]{:S(2)}) copy-start(f32[8]{0:T(128)} %param.10) | copy-start | bytes 100
  0.7 0.7 %copy-start.4 = (s32[64]{0:T(128)S(1)}, s32[64]{0:T(128)}, u32[]{:S(2)}) copy-start(s32[64]{0:T(128)} %param.11) | copy-start | bytes 772
  0.7 0.7 %copy-start.5 = (s32[4]{0:T(128)S(1)}, s32[4]{0:T(128)}, u32[]{:S(2)}) copy-start(s32[4]{0:T(128)} %param.12) | copy-start | bytes 52
  1.3 1.2 %copy-start = (f32[2,8,8,2048]{3,2,1,0:T(8,128)S(1)}, f32[2,8,8,2048]{3,2,1,0:T(8,128)}, u32[]{:S(2)}) copy-start(f32[2,8,8,2048]{3,2,1,0:T(8,128)} %f_hbm.1) | copy-start | bytes 3145732
  2.6 1.2 %copy-start.1 = (f32[2,8,8,2048]{3,2,1,0:T(8,128)S(1)}, f32[2,8,8,2048]{3,2,1,0:T(8,128)}, u32[]{:S(2)}) copy-start(f32[2,8,8,2048]{3,2,1,0:T(8,128)} %s_hbm.1) | copy-start | bytes 3145732
  3.8 0.8 %copy-start.2 = (f32[8,2048]{1,0:T(8,128)S(1)}, f32[8,2048]{1,0:T(8,128)}, u32[]{:S(2)}) copy-start(f32[8,2048]{1,0:T(8,128)} %eps_hbm.1) | copy-start | bytes 196612

commit v4 on v3

--- a/solution.py
+++ b/solution.py
@@ -188,13 +188,25 @@
     up, down = me - 1, me + 1
     has_up, has_down = me > 0, me < n - 1
 
-    load_f = pltpu.make_async_copy(f_hbm, f_in, load_sem.at[0])
+    load_f = [
+        pltpu.make_async_copy(f_hbm.at[c], f_in.at[c], load_sem.at[5 * c]) for c in range(2)
+    ]
     load_eps = pltpu.make_async_copy(eps_hbm, eps_in, load_sem.at[1])
-    load_s = [pltpu.make_async_copy(s_hbm.at[c], s_in.at[c], load_sem.at[2 + c]) for c in range(2)]
-    load_s[0].start()
-    load_s[1].start()
-    load_eps.start()
-    load_f.start()
+    half = waves // 2
+    load_s = [
+        [
+            pltpu.make_async_copy(
+                s_hbm.at[c, pl.ds(h * half, half)],
+                s_in.at[c, pl.ds(h * half, half)],
+                load_sem.at[6 + 2 * c + h],
+            )
+            for h in range(2)
+        ]
+        for c in range(2)
+    ]
+    for pair in load_s:
+        for load in pair:
+            load.start()
 
     barrier = pltpu.get_barrier_semaphore()
 
@@ -208,7 +220,8 @@
         return pl.ds(pl.multiple_of(b * LANES, LANES), LANES)
 
     for c in range(2):
-        load_s[c].wait()
+        load_s[c][0].wait()
+        load_s[c][1].wait()
 
         @pl.loop(0, blocks)
         def _(b):
@@ -268,6 +281,9 @@
         def _():
             to_down(i).wait_send()
 
+    load_eps.start()
+    load_f[0].start()
+    load_f[1].start()
     pl.semaphore_wait(barrier, n - 1)
     start(0)
 
@@ -288,7 +304,8 @@
         E[DEPTH + r] = eps_in[pl.ds(r, 1), :]
     start(1)
 
-    load_f.wait()
+    load_f[0].wait()
+    load_f[1].wait()
 
     @pl.loop(0, blocks)
     def _(b):
@@ -619,7 +636,7 @@
             pltpu.VMEM((n, rows, width), f32),
             pltpu.VMEM((n, rows, width), f32),
             pltpu.SMEM((n,), jnp.int32),
-            dma((4,)),
+            dma((10,)),
             dma((2 * DEPTH + 4,)),
             dma((2 * DEPTH + 4,)),
             dma((n,)),

time: 43.6 us -> 43.5 us (level)
  no operation moved by 1% of the time
where the time goes in v4:
time: 43.5 us; the launch traced here: 43.3 us
  Pallas kernels  37.1 us (85%)
  local copies, waits for them, and re-layouts  5.56 us (13%)
  between operations  0.68 us (2%)
    pallas_call x1, Pallas kernels, local(): pl.pallas_call(functools.partial(kernel, n), out_shape=(jax.ShapeDtypeStr...  37.1 us
    unnamed x16, local copies, waits for them, and re-layouts  5.56 us

profile of v4, /device:TPU:0, one launch (start us, length us, event | category | flops | bytes accessed | tf_op | source)
XLA Modules:
  0.0 43.3 jit_solution(2929712173533388143)
XLA Ops:
  0.6 0.0 copy-start.6
  0.6 0.0 copy-start.3
  0.7 0.0 copy-start.4
  0.7 0.0 copy-start.5
  0.7 0.6 %copy-done.6 = s32[1,16]{1,0:T(1,128)S(1)} copy-done((s32[1,16]{1,0:T(1,128)S(1)}, s32[1,16]{1,0:T(1,128)}, u32[]{:S(2)}) %copy-start.6) | copy-done | bytes 88
  1.3 0.0 copy-done.3
  1.3 0.0 copy-done.4
  1.3 0.0 copy-done.5
  1.3 0.0 copy-start
  1.3 1.2 %copy-done = f32[2,8,8,2048]{3,2,1,0:T(8,128)S(1)} copy-done((f32[2,8,8,2048]{3,2,1,0:T(8,128)S(1)}, f32[2,8,8,2048]{3,2,1,0:T(8,128)}, u32[]{:S(2)}) %copy-start) | copy-done | bytes 1048600
  2.6 0.0 copy-start.1
  2.6 1.2 %copy-done.1 = f32[2,8,8,2048]{3,2,1,0:T(8,128)S(1)} copy-done((f32[2,8,8,2048]{3,2,1,0:T(8,128)S(1)}, f32[2,8,8,2048]{3,2,1,0:T(8,128)}, u32[]{:S(2)}) %copy-start.1) | copy-done | bytes 1048600
  3.8 0.0 copy-start.2
  3.8 0.8 %copy-done.2 = f32[8,2048]{1,0:T(8,128)S(1)} copy-done((f32[8,2048]{1,0:T(8,128)S(1)}, f32[8,2048]{1,0:T(8,128)}, u32[]{:S(2)}) %copy-start.2) | copy-done | bytes 65560
  4.6 37.1 %shard_map.86 = (f32[2,8,8,2048]{3,2,1,0:T(8,128)S(1)}, f32[1,16,1024]{2,1,0:T(8,128)S(1)}) custom-call(f32[2,8,8,2048]{3,2,1,0:T(8,128)S(1)} %copy-done, f32[2,8,8,2048]{3,2,1,0:T(8,128)S(1)} %copy-done.1, f32[8,2048]{1,0:T(8,128)S(1)} %copy-done.2, f32[1,8]{1,0:T(1,128)S(1)} %bitcast.3, s32[1,64]{1,0:T(1,128)S(1)} %bitcast.4, s32[1,4]{1,0:T(1,128)S(1)} %bitcast.5, ...), custom_call_target="tpu_custom_call" | custom-call | tf_op jit(solution)/shard_map/pallas_call | solution.py:614
  41.7 1.0 %copy.11 = f32[2,8,8,2048]{3,2,1,0:T(8,128)} copy(f32[2,8,8,2048]{3,2,1,0:T(8,128)S(1)} %get-tuple-element.4) | data formatting | bytes 2097152
  42.7 0.6 %copy.12 = f32[1,16,1024]{2,1,0:T(8,128)} copy(f32[1,16,1024]{2,1,0:T(8,128)S(1)} %get-tuple-element.5) | data formatting | bytes 131072
Async XLA Ops:
  0.6 0.7 %copy-start.6 = (s32[1,16]{1,0:T(1,128)S(1)}, s32[1,16]{1,0:T(1,128)}, u32[]{:S(2)}) copy-start(s32[1,16]{1,0:T(1,128)} %owner_in.1) | copy-start | bytes 196
  0.6 0.7 %copy-start.3 = (f32[8]{0:T(128)S(1)}, f32[8]{0:T(128)}, u32[]{:S(2)}) copy-start(f32[8]{0:T(128)} %param.10) | copy-start | bytes 100
  0.7 0.7 %copy-start.4 = (s32[64]{0:T(128)S(1)}, s32[64]{0:T(128)}, u32[]{:S(2)}) copy-start(s32[64]{0:T(128)} %param.11) | copy-start | bytes 772
  0.7 0.7 %copy-start.5 = (s32[4]{0:T(128)S(1)}, s32[4]{0:T(128)}, u32[]{:S(2)}) copy-start(s32[4]{0:T(128)} %param.12) | copy-start | bytes 52
  1.3 1.2 %copy-start = (f32[2,8,8,2048]{3,2,1,0:T(8,128)S(1)}, f32[2,8,8,2048]{3,2,1,0:T(8,128)}, u32[]{:S(2)}) copy-start(f32[2,8,8,2048]{3,2,1,0:T(8,128)} %f_hbm.1) | copy-start | bytes 3145732
  2.6 1.2 %copy-start.1 = (f32[2,8,8,2048]{3,2,1,0:T(8,128)S(1)}, f32[2,8,8,2048]{3,2,1,0:T(8,128)}, u32[]{:S(2)}) copy-start(f32[2,8,8,2048]{3,2,1,0:T(8,128)} %s_hbm.1) | copy-start | bytes 3145732
  3.8 0.8 %copy-start.2 = (f32[8,2048]{1,0:T(8,128)S(1)}, f32[8,2048]{1,0:T(8,128)}, u32[]{:S(2)}) copy-start(f32[8,2048]{1,0:T(8,128)} %eps_hbm.1) | copy-start | bytes 196612
